TPU v7x, 32 devices: a whole 2x2x4 slice. The times are simulated.
32 devices in a mesh: energy: 8 (over z, x), atom: 4 (over y, core).
Axes of the slice: x: 2, y: 2, z: 4, core: 2. Of those that a mesh axis runs over, the one named last changes fastest.
Arguments:
- greens: bfloat16 [2, 64, 64, 256], P(None, ('energy', 'atom')), may hold values from -6 to 6
- coupling: bfloat16 [64, 8, 256], P('atom'), may hold values from -1.5 to 1.5
- neighbours: int32 [64, 8], P('atom'), may hold values from 0 to 63, as said below
- counts: int32 [64], P('atom'), may hold values from 4 to 8, as said below
- phonon_weights: float32 [2, 16], replicated, may hold values from 0.02 to 0.12
- offsets: int32 [16], replicated, may hold values from 1 to 8, as said below
Outputs:
- self_energy: bfloat16 [2, 64, 64, 256], P(None, 'energy', 'atom')
- phonon_self: float32 [64, 128], P('atom')
- current: float32 [64, 256], P(('energy', 'atom'))
Inputs may be any that keep to these rules, and one draw needn't show every extreme that they name: `neighbours`: every entry of row a differs from a by 1 to 8; in every draw some entry lies exactly 8 from its atom. Atom a uses its first counts[a] listed neighbours; every draw holds an atom with 8 and one with 4. `offsets`: every draw holds a shift of 1 and a shift of 8.
All inputs are finite; a program needn't handle non-finite values.
Results may differ from a plain program's by a relative error of at most 0.0067.
Values may be sent and summed in bfloat16 or wider, within the bound.
A program may use at most 64 MiB of HBM per device.

v0:
```python
import math

import jax
import jax.numpy as jnp
from jax import lax
from jax.sharding import PartitionSpec as P

NO = 16
NB = 8
NW = 16
REACH = 8


def with_halo(array, sides, width):
    for axis, dim in sides:
        size, length = (lax.axis_size(axis), array.shape[dim])
        up = [(i, (i + 1) % size) for i in range(size - 1)]
        down = [(j, i) for i, j in up]
        last = lax.slice_in_dim(array, length - width, length, axis=dim)
        leading = lax.slice_in_dim(array, 0, width, axis=dim)
        before = lax.ppermute(last, axis, up)
        after = lax.ppermute(leading, axis, down)
        array = jnp.concatenate([before, array, after], axis=dim)
    return array


def shift_tables(phonon_weights, offsets, energies, framed_rows):
    target = lax.broadcasted_iota(jnp.int32, (energies, framed_rows), 1)
    anchor = lax.broadcasted_iota(jnp.int32, (energies, framed_rows), 0)
    distance = (target - anchor - REACH)[None, :, :]
    shifts = offsets[:, None, None]
    upward = (distance == shifts).astype(jnp.float32)
    downward = (distance == -shifts).astype(jnp.float32)
    emission = phonon_weights[0][:, None, None]
    absorption = phonon_weights[1][:, None, None]
    table_less = jnp.sum(emission * upward + absorption * downward, axis=0)
    table_greater = jnp.sum(emission * downward + absorption * upward, axis=0)
    return (table_less.astype(jnp.bfloat16), table_greater.astype(jnp.bfloat16), upward)


def collision(sigma, green):
    energies = sigma.shape[1]
    atom_count = sigma.shape[2]
    sigma_blocks = sigma.reshape(2, energies, atom_count, NO, NO)
    green_blocks = green.reshape(2, energies, atom_count, NO, NO)
    gain = jnp.einsum(
        "eaij,eajk->eik", sigma_blocks[1], green_blocks[0], preferred_element_type=jnp.float32
    )
    loss = jnp.einsum(
        "eaij,eajk->eik", sigma_blocks[0], green_blocks[1], preferred_element_type=jnp.float32
    )
    return (gain - loss).reshape(energies, NO * NO)


def shards(greens, coupling, neighbours, counts, phonon_weights, offsets):
    energy_tile = lax.all_to_all(greens, "atom", split_axis=2, concat_axis=1, tiled=True)
    energies = energy_tile.shape[1]
    atom_count = energy_tile.shape[2]
    block_cells = energy_tile.shape[3]
    framed = with_halo(energy_tile, (("energy", 1), ("atom", 2)), REACH)
    framed_rows = energies + 2 * REACH
    table_less, table_greater, upward = shift_tables(phonon_weights, offsets, energies, framed_rows)
    mixed_less = jnp.einsum(
        "xy,ybc->xbc", table_less, framed[0], preferred_element_type=jnp.float32
    ).astype(jnp.bfloat16)
    mixed_greater = jnp.einsum(
        "xy,ybc->xbc", table_greater, framed[1], preferred_element_type=jnp.float32
    ).astype(jnp.bfloat16)
    sources = jnp.stack([mixed_less, mixed_greater, framed[1, REACH : REACH + energies]])
    own_less = framed[0, :, REACH : REACH + atom_count]
    atom_start = lax.axis_index("atom") * atom_count
    local_index = neighbours - atom_start + REACH
    total_energies = energies * lax.axis_size("energy")
    total_atoms = atom_count * lax.axis_size("atom")
    scale_phonon = 1.0 / math.sqrt(NO * NO * total_energies)
    scale_current = 1.0 / math.sqrt(NO * total_atoms)

    def slot_step(collected, slot_number):
        slot_index = lax.dynamic_index_in_dim(local_index, slot_number, 1, keepdims=False)
        active = (slot_number < counts).astype(jnp.float32)
        matrix = lax.dynamic_index_in_dim(coupling, slot_number, 1, keepdims=False).reshape(
            atom_count, NO, NO
        )
        gathered = jnp.take(sources, slot_index, axis=2).reshape(3, energies, atom_count, NO, NO)
        left_half = jnp.einsum(
            "aij,seajk->seaik", matrix, gathered, preferred_element_type=jnp.float32
        ).astype(jnp.bfloat16)
        sandwich = jnp.einsum(
            "seaik,alk->seail", left_half, matrix, preferred_element_type=jnp.float32
        )
        sandwich = sandwich.reshape(3, energies, atom_count, block_cells)
        collected = collected + sandwich[:2] * active[None, None, :, None]
        bubble = sandwich[2].astype(jnp.bfloat16)
        intersections = jnp.einsum(
            "xac,yac->axy", bubble, own_less, preferred_element_type=jnp.float32
        )
        phonon_term = jnp.sum(intersections[None] * upward[:, None], axis=(2, 3))
        return (collected, phonon_term * (active * scale_phonon)[None, :])

    initial = jnp.zeros((2, energies, atom_count, block_cells), jnp.float32)
    collected, terms = lax.scan(slot_step, initial, jnp.arange(NB, dtype=jnp.int32))
    self_energy = collected.astype(jnp.bfloat16)
    phonon_part = jnp.transpose(terms, (2, 0, 1)).reshape(atom_count, NB * NW)
    phonon_self = lax.psum(phonon_part, "energy")
    returned = lax.all_to_all(self_energy, "atom", split_axis=1, concat_axis=2, tiled=True)
    current = collision(returned, greens) * scale_current
    return (self_energy, phonon_self, current)


def solution(mesh):
    placed = (
        P(None, ("energy", "atom"), None, None),
        P("atom", None, None),
        P("atom", None),
        P("atom"),
        P(),
        P(),
    )
    return jax.shard_map(
        shards,
        mesh=mesh,
        in_specs=placed,
        out_specs=(P(None, "energy", "atom", None), P("atom", None), P(("energy", "atom"), None)),
        check_vma=False,
    )
```

profile of v0, /device:TPU:0, one launch (start us, length us, event | category | flops | bytes accessed | tf_op | source)
XLA Modules:
  0.0 244.4 jit_solution(15972045402336605702)
XLA Ops:
  2.3 4.2 %all-to-all-start = ((bf16[2,2,64,256]{3,1,0,2:T(2,128)(2,1)}), bf16[2,2,64,256]{3,1,0,2:T(2,128)(2,1)S(1)}, u32[]{:S(2)}, u32[]{:S(2)}) async-start(bf16[2,2,64,256]{3,1,0,2:T(2,128)(2,1)} %copy.47), calls=%async_computation | async-start | bytes 262144 | tf_op jit(solution)/shard_map/all_to_all | solution.py:56
  8.6 2.6 %all-to-all-done = bf16[2,2,64,256]{3,1,0,2:T(2,128)(2,1)S(1)} async-done(((bf16[2,2,64,256]{3,1,0,2:T(2,128)(2,1)}), bf16[2,2,64,256]{3,1,0,2:T(2,128)(2,1)S(1)}, u32[]{:S(2)}, u32[]{:S(2)}) %all-to-all-start) | async-done | bytes 131104 | tf_op jit(solution)/shard_map/all_to_all | solution.py:56
  11.4 3.9 %collective-permute-start = (bf16[2,8,16,256]{3,1,2,0:T(8,128)(2,1)S(1)}, bf16[2,8,16,256]{3,1,2,0:T(8,128)(2,1)S(1)}, u32[]{:S(2)}, u32[]{:S(2)}) collective-permute-start(bf16[2,8,16,256]{3,1,2,0:T(8,128)(2,1)S(1)} %all_to_all.27), channel_id=1, source_target_pairs={{0,4},{4,8},{8,12},{12,16},{16,20},{20,24},{24,28},{1,5},{5,9},{9,... | collective-permute-start | bytes 393224 | tf_op jit(solution)/shard_map/ppermute | solution.py:21
  19.6 5.5 %collective-permute-done.1 = bf16[2,8,16,256]{3,1,2,0:T(8,128)(2,1)S(1)} collective-permute-done((bf16[2,8,16,256]{3,1,2,0:T(8,128)(2,1)S(1)}, bf16[2,8,16,256]{3,1,2,0:T(8,128)(2,1)S(1)}, u32[]{:S(2)}, u32[]{:S(2)}) %collective-permute-start.1) | collective-permute-done | bytes 131104 | tf_op jit(solution)/shard_map/ppermute | solution.py:22
  28.5 2.0 collective-permute-done.3
  32.3 179.8 %while.13 = (s32[]{:T(128)}, f32[2,8,16,256]{3,2,1,0:T(8,128)S(1)}, f32[8,16,16]{2,1,0:T(8,128)}, s32[8]{0:T(128)}, bf16[16,8,256]{2,0,1:T(8,128)(2,1)}, /*index...) while((s32[]{:T(128)}, f32[2,8,16,256]{3,2,1,0:T(8,128)S(1)}, ...), condition=%wide.region_4.5_spmd.clone, body=%wide.region_2.4_spmd.clone.sunk | while | flops 8363174 | bytes 5939213 | solution.py:101
  35.7 1.9 compare_select_fusion.8
  44.8 2.4 convolution_bitcast_fusion.4
  58.2 1.9 compare_select_fusion.8
  67.3 2.4 convolution_bitcast_fusion.4
  80.7 1.9 compare_select_fusion.8
  89.8 2.4 convolution_bitcast_fusion.4
  103.1 1.9 compare_select_fusion.8
  112.2 2.4 convolution_bitcast_fusion.4
  125.6 1.9 compare_select_fusion.8
  134.7 2.4 convolution_bitcast_fusion.4
  148.1 1.9 compare_select_fusion.8
  157.2 2.4 convolution_bitcast_fusion.4
  170.6 1.9 compare_select_fusion.8
  179.7 2.4 convolution_bitcast_fusion.4
  193.0 1.9 compare_select_fusion.8
  202.1 2.4 convolution_bitcast_fusion.4
  212.8 5.4 %all-to-all-start.1 = ((bf16[2,8,16,256]{3,2,0,1:T(8,128)(2,1)}), bf16[2,8,16,256]{3,2,0,1:T(8,128)(2,1)S(1)}, u32[]{:S(2)}, u32[]{:S(2)}) async-start(bf16[2,8,16,256]{3,2,0,1:T(8,128)(2,1)} %copy.68), calls=%async_computation.1 | async-start | bytes 262144 | tf_op jit(solution)/shard_map/all_to_all | solution.py:105
  221.0 20.6 %psum.7 = f32[16,128]{1,0:T(8,128)} all-reduce(f32[16,128]{1,0:T(8,128)S(1)} %copy.62), channel_id=1, replica_groups=mesh['energy'=8,'atom'=4] {'energy'}, use_global_device_ids=true, to_apply=%region_5.6 | all-reduce | flops 2048 | bytes 16384 | tf_op jit(solution)/shard_map/psum | solution.py:104
  (254 shorter events, 147.2 us)
Async XLA Ops:
  2.3 8.9 %all-to-all-start = ((bf16[2,2,64,256]{3,1,0,2:T(2,128)(2,1)}), bf16[2,2,64,256]{3,1,0,2:T(2,128)(2,1)S(1)}, u32[]{:S(2)}, u32[]{:S(2)}) async-start(bf16[2,2,64,256]{3,1,0,2:T(2,128)(2,1)} %copy.47), calls=%async_computation | async-start | bytes 262144 | tf_op jit(solution)/shard_map/all_to_all | solution.py:56
  11.4 8.2 %collective-permute-start = (bf16[2,8,16,256]{3,1,2,0:T(8,128)(2,1)S(1)}, bf16[2,8,16,256]{3,1,2,0:T(8,128)(2,1)S(1)}, u32[]{:S(2)}, u32[]{:S(2)}) collective-permute-start(bf16[2,8,16,256]{3,1,2,0:T(8,128)(2,1)S(1)} %all_to_all.27), channel_id=1, source_target_pairs={{0,4},{4,8},{8,12},{12,16},{16,20},{20,24},{24,28},{1,5},{5,9},{9,... | collective-permute-start | bytes 393224 | tf_op jit(solution)/shard_map/ppermute | solution.py:21
  18.2 6.9 %collective-permute-start.1 = (bf16[2,8,16,256]{3,1,2,0:T(8,128)(2,1)S(1)}, bf16[2,8,16,256]{3,1,2,0:T(8,128)(2,1)S(1)}, u32[]{:S(2)}, u32[]{:S(2)}) collective-permute-start(bf16[2,8,16,256]{3,1,2,0:T(8,128)(2,1)S(1)} %all_to_all.27), channel_id=1, source_target_pairs={{4,0},{8,4},{12,8},{16,12},{20,16},{24,20},{28,24},{5,1},{9,5},{13... | collective-permute-start | bytes 393224 | tf_op jit(solution)/shard_map/ppermute | solution.py:22
  25.2 3.3 %collective-permute-start.2 = (bf16[2,24,8,256]{3,1,2,0:T(8,128)(2,1)S(1)}, bf16[2,24,8,256]{3,1,2,0:T(8,128)(2,1)S(1)}, u32[]{:S(2)}, u32[]{:S(2)}) collective-permute-start(bf16[2,24,8,256]{3,1,2,0:T(8,128)(2,1)S(1)} %get-tuple-element.174), channel_id=1, source_target_pairs={{0,1},{1,2},{2,3},{4,5},{5,6},{6,7},{8,9},{9,10},{10,11},{12,13},{... | collective-permute-start | bytes 589832 | tf_op jit(solution)/shard_map/ppermute | solution.py:21
  26.5 4.0 %collective-permute-start.3 = (bf16[2,24,8,256]{3,1,2,0:T(8,128)(2,1)S(1)}, bf16[2,24,8,256]{3,1,2,0:T(8,128)(2,1)S(1)}, u32[]{:S(2)}, u32[]{:S(2)}) collective-permute-start(bf16[2,24,8,256]{3,1,2,0:T(8,128)(2,1)S(1)} %get-tuple-element.175), channel_id=1, source_target_pairs={{1,0},{2,1},{3,2},{5,4},{6,5},{7,6},{9,8},{10,9},{11,10},{13,12},{... | collective-permute-start | bytes 589832 | tf_op jit(solution)/shard_map/ppermute | solution.py:22
  30.5 1.8 copy-start.3
  51.6 1.1 copy-start
  52.6 1.6 copy-start.4
  74.1 1.1 copy-start
  75.1 1.6 copy-start.4
  96.6 1.1 copy-start
  97.5 1.6 copy-start.4
  119.0 1.1 copy-start
  120.0 1.6 copy-start.4
  141.5 1.1 copy-start
  142.5 1.6 copy-start.4
  164.0 1.1 copy-start
  165.0 1.6 copy-start.4
  186.5 1.1 copy-start
  187.4 1.6 copy-start.4
  209.0 1.1 copy-start
  209.9 1.6 copy-start.4
  212.1 8.8 %copy-start.2 = (f32[8,16,16]{2,1,0:T(8,128)S(1)}, f32[8,16,16]{2,1,0:T(8,128)}, u32[]{:S(2)}) copy-start(f32[8,16,16]{2,1,0:T(8,128)} %get-tuple-element.57) | copy-start | bytes 24580
  212.8 28.8 %all-to-all-start.1 = ((bf16[2,8,16,256]{3,2,0,1:T(8,128)(2,1)}), bf16[2,8,16,256]{3,2,0,1:T(8,128)(2,1)S(1)}, u32[]{:S(2)}, u32[]{:S(2)}) async-start(bf16[2,8,16,256]{3,2,0,1:T(8,128)(2,1)} %copy.68), calls=%async_computation.1 | async-start | bytes 262144 | tf_op jit(solution)/shard_map/all_to_all | solution.py:105
  (8 other events, 7.6 us)
where the time goes:
time: 247 us; the launch traced here: 244 us
  local copies, waits for them, and re-layouts  111 us (45%)
  other arithmetic  45.7 us (19%)
  matrix products  21.5 us (9%)
  blocking collectives  20.6 us (8%)
  starting transfers between devices  17.5 us (7%)
  loops' own time  17.2 us (7%)
  waiting for transfers between devices  10.1 us (4%)
    slice x24, local copies, waits for them, and re-layouts, slot_step(): collected = collected + sandwich[:2] * active[None, None, :, None]  35.1 us
    gather x24, local copies, waits for them, and re-layouts, slot_step(): jnp.take(sources, slot_index, axis=2)  33.7 us
    psum x1, blocking collectives, shards(): phonon_self = lax.psum(phonon_part, 'energy')  20.6 us
    dot_general x8, matrix products, slot_step(): jnp.einsum('seaik,alk->seail', left_half, matrix, preferred_element_type=...  19.5 us
    another operation x1, loops' own time, shards(): lax.scan(slot_step, initial, jnp.arange(NB, dtype=jnp.int32))  17.2 us
    mul x8, other arithmetic, slot_step(): return (collected, phonon_term * (active * scale_phonon)[None, :])  15.4 us
    convert_element_type x8, other arithmetic, slot_step(): active = (slot_number < counts).astype(jnp.float32)  10.7 us
    dynamic_slice x8, local copies, waits for them, and re-layouts, shards(): lax.scan(slot_step, initial, jnp.arange(NB, dtype=jnp.int32))  10.6 us
  transfers between devices with their start and end apart: 6, of which 3 were waited for; matrix products, arithmetic and copies ran while one was open for 3% of the time, Pallas kernels for 0%

commit v1 on v0

v1 whole, which is shorter than its diff:
```python
import functools
import math

import jax
import jax.numpy as jnp
from jax import lax
from jax.experimental import pallas as pl
from jax.experimental.pallas import tpu as pltpu
from jax.sharding import PartitionSpec as P

NO = 16
REACH = 8
LANES = 128
MESH = pl.DeviceIdType.MESH


def iota(shape, dim):
    return lax.broadcasted_iota(jnp.int32, shape, dim)


def kernel(
    n_e, n_a,
    greens, coupling, neighbours, counts, weights, offsets,
    sigma_out, phonon_out, current_out,
    spread, sendbuf, recv, framed, left, right, kron, sources,
    sums, inter, pre, mine_p, got_p, mine_c, got_c,
    send_sem, recv_sem, own_sem, psend, precv, csend, crecv,
):
    _, rows, all_atoms, cells = greens.shape
    atoms, slots = neighbours.shape
    edges = atoms * slots
    width = n_a * rows
    span = width + 2 * REACH
    planes = 2 * rows
    window = atoms + 2 * REACH
    chunks = window // REACH
    halves = cells // LANES
    line = 2 * window
    ei = lax.axis_index("energy")
    ai = lax.axis_index("atom")
    lower = ei > 0
    upper = ei < n_e - 1
    f32, bf16 = jnp.float32, jnp.bfloat16

    def ok(d):
        return {-1: lower, 1: upper}.get(d)

    def guarded(d, body):
        if d == 0:
            body()
        else:
            pl.when(ok(d))(body)

    barrier = pltpu.get_barrier_semaphore()

    def greet(e, a):
        pl.semaphore_signal(barrier, inc=1, device_id=(e, a), device_id_type=MESH)

    for d in (-1, 0, 1):
        for k in range(n_a):
            if d or k:
                guarded(d, lambda d=d, k=k: greet(ei + d, lax.rem(ai + k, n_a)))

    def greet_far(k, carry):
        other = lax.rem(ei + k, n_e)
        pl.when((other != ei - 1) & (other != ei + 1))(lambda: greet(other, ai))
        return carry

    lax.fori_loop(1, n_e, greet_far, 0)

    stretch = 2 * all_atoms
    for plane in range(planes):
        for h in range(halves):
            spread[pl.ds(plane * stretch + h, all_atoms, stride=2), :] = greens[
                plane // rows, plane % rows, :, h * LANES:(h + 1) * LANES
            ].astype(f32)
    none = jnp.zeros((2 * REACH, LANES), bf16)
    for plane in range(planes):
        sendbuf[plane, 0] = none
        sendbuf[plane, all_atoms // REACH + 1] = none
        sendbuf[plane, 1:all_atoms // REACH + 1] = (
            spread[plane * stretch:(plane + 1) * stretch, :]
            .astype(bf16).reshape(all_atoms // REACH, 2 * REACH, LANES)
        )

    near = lower.astype(jnp.int32) + upper.astype(jnp.int32)
    pl.semaphore_wait(barrier, n_a - 1 + n_a * near + (n_e - 1 - near))

    step = atoms // REACH

    def block_copy(d, k):
        other = lax.rem(ai + k, n_a)
        slot = (1 - d) * n_a + ai
        return pltpu.make_async_remote_copy(
            src_ref=sendbuf.at[:, pl.ds(step * other, chunks)],
            dst_ref=recv.at[slot],
            send_sem=send_sem.at[(d + 1) * n_a + k],
            recv_sem=recv_sem.at[slot],
            device_id=(ei + d, other),
            device_id_type=MESH,
        )

    for k in range(n_a - 1, -1, -1):
        for d in (-1, 1, 0):
            if d or k:
                guarded(d, lambda d=d, k=k: block_copy(d, k).start())
    own = pltpu.make_async_copy(
        sendbuf.at[:, pl.ds(step * ai, chunks)], recv.at[n_a + ai], own_sem
    )
    own.start()

    def clear(first):
        for k in range(n_a):
            recv[first + k] = jnp.zeros(recv.shape[1:], bf16)

    pl.when(jnp.logical_not(lower))(lambda: clear(0))
    pl.when(jnp.logical_not(upper))(lambda: clear(2 * n_a))

    big_row, big_col = iota((cells, cells), 0), iota((cells, cells), 1)
    same_block = (big_row // NO == big_col // NO).astype(f32).astype(bf16)
    same_place = (big_row // NO == big_col % NO).astype(f32).astype(bf16)
    flat = coupling[...].reshape(edges, cells).astype(f32)
    place = iota((edges, cells), 1) % NO

    def expand(j, carry):
        picked = jnp.where(place == j, flat, 0.0).astype(bf16)
        one = jnp.dot(picked, same_block, preferred_element_type=f32)
        two = jnp.dot(picked, same_place, preferred_element_type=f32)
        for h in range(halves):
            at = pl.ds(pl.multiple_of((h * NO + j) * edges, edges), edges)
            left[at, :] = one[:, h * LANES:(h + 1) * LANES]
            right[at, :] = two[:, h * LANES:(h + 1) * LANES]
        return carry

    lax.fori_loop(0, NO, expand, 0)

    def product(edge, carry):
        for h in range(halves):
            block = right[pl.ds(h * NO * edges + edge, NO, stride=edges), :]
            for j in range(NO):
                row = left[pl.ds((h * NO + j) * edges + edge, 1), :]
                kron[edge, j * NO:(j + 1) * NO, h * LANES:(h + 1) * LANES] = (
                    jnp.broadcast_to(row, (NO, LANES)) * block
                ).astype(bf16)
        return carry

    lax.fori_loop(0, edges, product, 0)

    shape = (6 * width, 2 * span)
    row, col = iota(shape, 0), iota(shape, 1)
    kind = row // width
    half = (col // rows) % 2
    energy = (col // planes) * rows + col % rows
    distance = energy - row % width - REACH
    shift = jnp.where(kind == 0, distance, -distance)
    coef = jnp.zeros(shape, f32)
    for w in range(offsets.shape[0]):
        coef = coef + jnp.where(shift == offsets[w], weights[0, w], 0.0)
        coef = coef + jnp.where(shift == -offsets[w], weights[1, w], 0.0)
    middle = jnp.where((kind == 2) & (half == 1) & (distance == 0), 1.0, 0.0)
    above = jnp.where((kind >= 4) & (half == 0) & (energy - REACH == row - 4 * width), 1.0, 0.0)
    table = jnp.where((kind < 2) & (kind == half), coef, middle + above).astype(bf16)

    own.wait()
    for d in (-1, 0, 1):
        for k in range(n_a):
            if d or k:
                def arrive(d=d, k=k):
                    slot = (d + 1) * n_a + lax.rem(ai + k, n_a)
                    pltpu.make_async_remote_copy(
                        src_ref=sendbuf.at[:, pl.ds(0, chunks)],
                        dst_ref=recv.at[slot],
                        send_sem=send_sem.at[(d + 1) * n_a + k],
                        recv_sem=recv_sem.at[slot],
                        device_id=(ei + d, lax.rem(ai + k, n_a)),
                        device_id_type=MESH,
                    ).wait()
                guarded(d, arrive)

    def widen(position, carry):
        for plane in range(planes):
            at = pl.multiple_of((position * planes + plane) * line, line)
            framed[pl.ds(at, line), :] = recv[position, plane].reshape(line, LANES).astype(f32)
        return carry

    lax.fori_loop(0, 3 * n_a, widen, 0)

    def mix(t, carry):
        for h in range(halves):
            column = framed[pl.ds(2 * t + h, 2 * span, stride=line), :].astype(bf16)
            sources[t, :, h * LANES:(h + 1) * LANES] = jnp.dot(
                table, column, preferred_element_type=f32
            ).astype(bf16)
        return carry

    lax.fori_loop(0, window, mix, 0)

    first = ai * atoms - REACH
    both = 2 * width

    def atom_step(a, carry):
        total = jnp.zeros((both, cells), f32)
        bubbles = []
        for n in range(slots):
            place = jnp.clip(neighbours[a, n] - first, 0, window - 1)
            mixed = sources[place, 0:4 * width, :]
            result = jnp.dot(mixed, kron[a * slots + n], preferred_element_type=f32)
            live = jnp.where(n < counts[a], 1.0, 0.0)
            total = total + result[:both] * live
            bubbles.append(result[both:both + width])
        bubble = jnp.concatenate(bubbles, axis=0).astype(bf16)
        inter[pl.ds(pl.multiple_of(a * slots * width, slots * width), slots * width), 0:both] = (
            lax.dot_general(
                bubble, sources[REACH + a, 4 * width:6 * width, :],
                (((1,), (1,)), ((), ())), preferred_element_type=f32,
            )
        )
        for h in range(halves):
            sums[pl.ds(h * both * atoms + a, both, stride=atoms), :] = total[
                :, h * LANES:(h + 1) * LANES
            ]
        return carry

    inter[...] = jnp.zeros(inter.shape, f32)
    lax.fori_loop(0, atoms, atom_step, 0)

    by_shift = jnp.zeros((edges, LANES), f32)
    for e in range(width):
        part = inter[pl.ds(e, edges, stride=width), :]
        by_shift = by_shift + pltpu.roll(part, (LANES - e - 1) % LANES, 1)
    mine_p[...] = by_shift.T[0:REACH, :]

    def phonon_copy(k):
        other = lax.rem(ei + k, n_e)
        return pltpu.make_async_remote_copy(
            src_ref=mine_p, dst_ref=got_p.at[ei],
            send_sem=psend.at[k], recv_sem=precv.at[ei],
            device_id=(other, ai), device_id_type=MESH,
        )

    def phonon_send(k, carry):
        phonon_copy(k).start()
        return carry

    lax.fori_loop(1, n_e, phonon_send, 0)

    place = iota((NO, cells), 1) % NO
    for e in range(width):
        sig, gre = [], []
        for s in (1, 0):
            parts = []
            for h in range(halves):
                at = (h * both + s * width + e) * atoms
                value = sums[at:at + atoms, :].astype(bf16)
                sigma_out[s, e, :, h * LANES:(h + 1) * LANES] = value
                parts.append(value)
            sig.append(jnp.concatenate(parts, axis=1))
        for g in range(2):
            base = ((n_a + e // rows) * planes + g * rows + e % rows) * line + 2 * REACH
            gre.append(jnp.concatenate(
                [framed[pl.ds(base + h, atoms, stride=2), :].astype(bf16) for h in range(halves)],
                axis=1,
            ))
        outer = lax.dot_general(
            jnp.concatenate(gre, axis=0), jnp.concatenate([sig[0], -sig[1]], axis=0),
            (((0,), (0,)), ((), ())), preferred_element_type=f32,
        )
        chosen = jnp.zeros((NO, cells), f32)
        for j in range(NO):
            chosen = jnp.where(place == j, outer[j * NO:(j + 1) * NO, :], chosen)
        pre[e * NO:(e + 1) * NO, :] = chosen
    value = pre[...]
    high = value.astype(bf16)
    low = (value - high.astype(f32)).astype(bf16)
    wide = jnp.dot(high, same_block, preferred_element_type=f32)
    wide = wide + jnp.dot(low, same_block, preferred_element_type=f32)
    keep = iota((width * NO, cells), 0) % NO == iota((width * NO, cells), 1) % NO
    wide = jnp.where(keep, wide, 0.0).reshape(width, NO, cells)
    share = jnp.sum(wide, axis=1) * (1.0 / math.sqrt(NO * all_atoms))
    mine_c[...] = share

    def current_copy(k):
        other = lax.rem(ai + k, n_a)
        return pltpu.make_async_remote_copy(
            src_ref=mine_c, dst_ref=got_c.at[ai],
            send_sem=csend.at[k], recv_sem=crecv.at[ai],
            device_id=(ei, other), device_id_type=MESH,
        )

    for k in range(1, n_a):
        current_copy(k).start()

    def phonon_wait(k, total):
        slot = lax.rem(ei + k, n_e)
        pltpu.make_async_remote_copy(
            src_ref=mine_p, dst_ref=got_p.at[slot],
            send_sem=psend.at[k], recv_sem=precv.at[slot],
            device_id=(slot, ai), device_id_type=MESH,
        ).wait()
        return total + got_p[slot]

    found = lax.fori_loop(1, n_e, phonon_wait, mine_p[...])
    count_w = offsets.shape[0]
    lanes = slots * count_w
    frequency = iota((REACH, lanes), 1) % count_w
    wanted = jnp.zeros((REACH, lanes), jnp.int32)
    for w in range(count_w):
        wanted = jnp.where(frequency == w, offsets[w], wanted)
    select = (wanted - 1 == iota((REACH, lanes), 0)).astype(f32)
    tall = found.T
    picked = jnp.zeros((edges, lanes), f32)
    for k in range(REACH):
        picked = picked + tall[:, k:k + 1] * select[k:k + 1, :]
    keep = iota((edges, lanes), 0) % slots == iota((edges, lanes), 1) // count_w
    picked = jnp.sum(jnp.where(keep, picked, 0.0).reshape(atoms, slots, lanes), axis=1)
    used = jnp.zeros((atoms, lanes), jnp.int32)
    which = iota((atoms, lanes), 0)
    for a in range(atoms):
        used = jnp.where(which == a, counts[a], used)
    live = iota((atoms, lanes), 1) // count_w < used
    phonon_out[...] = jnp.where(live, picked * (1.0 / math.sqrt(cells * width * n_e)), 0.0)

    total = mine_c[...]
    for k in range(1, n_a):
        slot = lax.rem(ai + k, n_a)
        pltpu.make_async_remote_copy(
            src_ref=mine_c, dst_ref=got_c.at[slot],
            send_sem=csend.at[k], recv_sem=crecv.at[slot],
            device_id=(ei, slot), device_id_type=MESH,
        ).wait()
        total = total + got_c[slot]
    own_rows = total[0:rows]
    for k in range(1, n_a):
        own_rows = jnp.where(ai == k, total[k * rows:(k + 1) * rows], own_rows)
    current_out[...] = own_rows


def shards(n_e, n_a, greens, coupling, neighbours, counts, phonon_weights, offsets):
    _, rows, all_atoms, cells = greens.shape
    atoms, slots = neighbours.shape
    edges = atoms * slots
    width = n_a * rows
    span = width + 2 * REACH
    window = atoms + 2 * REACH
    chunks = window // REACH
    f32, bf16 = jnp.float32, jnp.bfloat16
    halves = cells // LANES
    vmem = pl.BlockSpec(memory_space=pltpu.VMEM)
    smem = pl.BlockSpec(memory_space=pltpu.SMEM)
    dma = pltpu.SemaphoreType.DMA
    return pl.pallas_call(
        functools.partial(kernel, n_e, n_a),
        out_shape=(
            jax.ShapeDtypeStruct((2, width, atoms, cells), bf16),
            jax.ShapeDtypeStruct((atoms, slots * offsets.shape[0]), f32),
            jax.ShapeDtypeStruct((rows, cells), f32),
        ),
        in_specs=[vmem, vmem, smem, smem, smem, smem],
        out_specs=(vmem, vmem, vmem),
        scratch_shapes=[
            pltpu.VMEM((2 * rows * 2 * all_atoms, LANES), f32),
            pltpu.VMEM((2 * rows, all_atoms // REACH + 2, 2 * REACH, LANES), bf16),
            pltpu.VMEM((3 * n_a, 2 * rows, chunks, 2 * REACH, LANES), bf16),
            pltpu.VMEM((2 * span * 2 * window, LANES), f32),
            pltpu.VMEM((halves * NO * edges, LANES), f32),
            pltpu.VMEM((halves * NO * edges, LANES), f32),
            pltpu.VMEM((edges, cells, cells), bf16),
            pltpu.VMEM((window, 6 * width, cells), bf16),
            pltpu.VMEM((halves * 2 * width * atoms, LANES), f32),
            pltpu.VMEM((edges * width, LANES), f32),
            pltpu.VMEM((width * NO, cells), f32),
            pltpu.VMEM((REACH, edges), f32),
            pltpu.VMEM((n_e, REACH, edges), f32),
            pltpu.VMEM((width, cells), f32),
            pltpu.VMEM((n_a, width, cells), f32),
            dma((3 * n_a,)), dma((3 * n_a,)), dma,
            dma((n_e,)), dma((n_e,)), dma((n_a,)), dma((n_a,)),
        ],
        compiler_params=pltpu.CompilerParams(
            collective_id=0, has_side_effects=True, vmem_limit_bytes=48 * 1024 * 1024
        ),
    )(greens, coupling, neighbours, counts, phonon_weights, offsets)


def solution(mesh):
    placed = (
        P(None, ("energy", "atom"), None, None),
        P("atom", None, None),
        P("atom", None),
        P("atom"),
        P(),
        P(),
    )
    return jax.shard_map(
        functools.partial(shards, mesh.shape["energy"], mesh.shape["atom"]),
        mesh=mesh,
        in_specs=placed,
        out_specs=(P(None, "energy", "atom", None), P("atom", None), P(("energy", "atom"), None)),
        check_vma=False,
    )
```

time: 247 us -> 40.7 us (0.16)
  local copies, waits for them, and re-layouts: 111 us -> 4.36 us
  other arithmetic: 45.7 us -> 0 us
  Pallas kernels: 0 us -> 35.5 us
  matrix products: 21.5 us -> 0 us
  blocking collectives: 20.6 us -> 0 us
  starting transfers between devices: 17.5 us -> 0 us
  loops' own time: 17.2 us -> 0 us
  waiting for transfers between devices: 10.1 us -> 0 us
    slice x37 -> x0, local copies, waits for them, and re-layouts: 43.5 us -> none  [the longest x24 35.1 us: slot_step(): collected = collected + sandwich[:2] * active[None, None, :, None]]
    pallas_call x0 -> x1, Pallas kernels: none -> 35.5 us  [shards(): pl.pallas_call(functools.partial(kernel, n_e, n_a), out_shape=(jax.ShapeD...]
    gather x24 -> x0, local copies, waits for them, and re-layouts: 33.7 us -> none  [slot_step(): jnp.take(sources, slot_index, axis=2)]
    dot_general x20 -> x0, matrix products: 21.5 us -> none  [the longest x8 19.5 us: slot_step(): jnp.einsum('seaik,alk->seail', left_half, matrix, preferred_element_type=...]
    psum x1 -> x0, blocking collectives: 20.6 us -> none  [shards(): phonon_self = lax.psum(phonon_part, 'energy')]
    another operation x1 -> x0, loops' own time: 17.2 us -> none  [shards(): lax.scan(slot_step, initial, jnp.arange(NB, dtype=jnp.int32))]
    dynamic_slice x16 -> x0, local copies, waits for them, and re-layouts: 16.2 us -> none  [the longest x8 10.6 us: shards(): lax.scan(slot_step, initial, jnp.arange(NB, dtype=jnp.int32))]
    mul x8 -> x0, other arithmetic: 15.4 us -> none  [slot_step(): return (collected, phonon_term * (active * scale_phonon)[None, :])]
  transfers between devices with their start and end apart: 6 -> 0, of which waited for: 3 -> 0; matrix products, arithmetic and copies ran while one was open for 3% -> 0% of each run, Pallas kernels for 0% -> 0%
where the time goes in v1:
time: 40.7 us; the launch traced here: 40.5 us
  Pallas kernels  35.5 us (87%)
  local copies, waits for them, and re-layouts  4.36 us (11%)
  between operations  0.68 us (2%)
    pallas_call x1, Pallas kernels, shards(): pl.pallas_call(functools.partial(kernel, n_e, n_a), out_shape=(jax.ShapeD...  35.5 us
    unnamed x14, local copies, waits for them, and re-layouts  4.36 us

profile of v1, /device:TPU:0, one launch (start us, length us, event | category | flops | bytes accessed | tf_op | source)
XLA Modules:
  0.0 40.5 jit_solution(16400482522655014209)
XLA Ops:
  0.6 0.0 copy-start.4
  0.6 0.0 copy-start.2
  0.7 0.0 copy-start.3
  0.7 0.8 %copy.9.neighbours = s32[16,8]{1,0:T(8,128)S(1)} copy(s32[16,8]{0,1:T(8,128)} %param.8) | data formatting | bytes 1024 | tf_op args[2]
  1.4 0.0 copy-done.4
  1.4 0.0 copy-done.2
  1.4 0.0 copy-done.3
  1.4 0.0 copy-start
  1.5 0.9 %copy-done = bf16[2,2,64,256]{3,2,1,0:T(8,128)(2,1)S(1)} copy-done((bf16[2,2,64,256]{3,2,1,0:T(8,128)(2,1)S(1)}, bf16[2,2,64,256]{3,2,1,0:T(8,128)(2,1)}, u32[]{:S(2)}) %copy-start) | copy-done | bytes 131096
  2.4 0.0 copy-start.1
  2.4 0.8 %copy-done.1 = bf16[16,8,256]{2,1,0:T(8,128)(2,1)S(1)} copy-done((bf16[16,8,256]{2,1,0:T(8,128)(2,1)S(1)}, bf16[16,8,256]{2,1,0:T(8,128)(2,1)}, u32[]{:S(2)}) %copy-start.1) | copy-done | bytes 65560
  3.2 35.5 %shard_map.85 = (bf16[2,8,16,256]{3,2,1,0:T(8,128)(2,1)S(1)}, f32[16,128]{1,0:T(8,128)S(1)}, f32[2,256]{1,0:T(2,128)S(1)}) custom-call(bf16[2,2,64,256]{3,2,1,0:T(8,128)(2,1)S(1)} %copy-done, bf16[16,8,256]{2,1,0:T(8,128)(2,1)S(1)} %copy-done.1, s32[16,8]{1,0:T(8,128)S(1)} %copy.9.neighbours, s32[16]{0:T(128)S(1)} %copy-done.3, f32[2,16]{1,0:T(2,128)S(1)} %copy-done.2, ...), custom_call_target="tpu_custom_call" | custom-call | tf_op jit(solution)/shard_map/pallas_call | solution.py:351
  38.7 0.7 %copy.13 = bf16[2,8,16,256]{3,2,1,0:T(8,128)(2,1)} copy(bf16[2,8,16,256]{3,2,1,0:T(8,128)(2,1)S(1)} %get-tuple-element.6) | data formatting | bytes 262144
  39.3 0.6 %copy.14 = f32[16,128]{1,0:T(8,128)} copy(f32[16,128]{1,0:T(8,128)S(1)} %get-tuple-element.7) | data formatting | bytes 16384
  39.9 0.6 %copy.15 = f32[2,256]{1,0:T(2,128)} copy(f32[2,256]{1,0:T(2,128)S(1)} %get-tuple-element.8) | data formatting | bytes 4096
Async XLA Ops:
  0.6 0.8 %copy-start.4 = (s32[16]{0:T(128)S(1)}, s32[16]{0:T(128)}, u32[]{:S(2)}) copy-start(s32[16]{0:T(128)} %offsets.1) | copy-start | bytes 196
  0.6 0.8 %copy-start.2 = (f32[2,16]{1,0:T(2,128)S(1)}, f32[2,16]{1,0:T(2,128)}, u32[]{:S(2)}) copy-start(f32[2,16]{1,0:T(2,128)} %weights.1) | copy-start | bytes 388
  0.7 0.8 %copy-start.3 = (s32[16]{0:T(128)S(1)}, s32[16]{0:T(128)}, u32[]{:S(2)}) copy-start(s32[16]{0:T(128)} %counts.1) | copy-start | bytes 196
  1.4 0.9 %copy-start = (bf16[2,2,64,256]{3,2,1,0:T(8,128)(2,1)S(1)}, bf16[2,2,64,256]{3,2,1,0:T(8,128)(2,1)}, u32[]{:S(2)}) copy-start(bf16[2,2,64,256]{3,2,1,0:T(8,128)(2,1)} %greens.1) | copy-start | bytes 393220
  2.4 0.8 %copy-start.1 = (bf16[16,8,256]{2,1,0:T(8,128)(2,1)S(1)}, bf16[16,8,256]{2,1,0:T(8,128)(2,1)}, u32[]{:S(2)}) copy-start(bf16[16,8,256]{2,1,0:T(8,128)(2,1)} %coupling.1) | copy-start | bytes 196612

commit v2 on v1

--- a/solution.py
+++ b/solution.py
@@ -22,20 +22,19 @@
     n_e, n_a,
     greens, coupling, neighbours, counts, weights, offsets,
     sigma_out, phonon_out, current_out,
-    spread, sendbuf, recv, framed, left, right, kron, sources,
+    local_coupling, recv, framed, left, right, kron, sources, higher,
     sums, inter, pre, mine_p, got_p, mine_c, got_c,
-    send_sem, recv_sem, own_sem, psend, precv, csend, crecv,
+    send_sem, recv_sem, own_sem, esend, erecv, psend, precv, csend, crecv,
 ):
     _, rows, all_atoms, cells = greens.shape
-    atoms, slots = neighbours.shape
+    slots, atoms = neighbours.shape
     edges = atoms * slots
     width = n_a * rows
     span = width + 2 * REACH
     planes = 2 * rows
     window = atoms + 2 * REACH
-    chunks = window // REACH
     halves = cells // LANES
-    line = 2 * window
+    line = halves * atoms
     ei = lax.axis_index("energy")
     ai = lax.axis_index("atom")
     lower = ei > 0
@@ -68,31 +67,20 @@
 
     lax.fori_loop(1, n_e, greet_far, 0)
 
-    stretch = 2 * all_atoms
-    for plane in range(planes):
-        for h in range(halves):
-            spread[pl.ds(plane * stretch + h, all_atoms, stride=2), :] = greens[
-                plane // rows, plane % rows, :, h * LANES:(h + 1) * LANES
-            ].astype(f32)
-    none = jnp.zeros((2 * REACH, LANES), bf16)
-    for plane in range(planes):
-        sendbuf[plane, 0] = none
-        sendbuf[plane, all_atoms // REACH + 1] = none
-        sendbuf[plane, 1:all_atoms // REACH + 1] = (
-            spread[plane * stretch:(plane + 1) * stretch, :]
-            .astype(bf16).reshape(all_atoms // REACH, 2 * REACH, LANES)
-        )
-
     near = lower.astype(jnp.int32) + upper.astype(jnp.int32)
     pl.semaphore_wait(barrier, n_a - 1 + n_a * near + (n_e - 1 - near))
 
-    step = atoms // REACH
+    coupling_copy = pltpu.make_async_copy(coupling, local_coupling, own_sem.at[1])
+    coupling_copy.start()
+
+    def part(other):
+        return greens.at[:, :, pl.ds(pl.multiple_of(other * atoms, atoms), atoms), :]
 
     def block_copy(d, k):
         other = lax.rem(ai + k, n_a)
         slot = (1 - d) * n_a + ai
         return pltpu.make_async_remote_copy(
-            src_ref=sendbuf.at[:, pl.ds(step * other, chunks)],
+            src_ref=part(other),
             dst_ref=recv.at[slot],
             send_sem=send_sem.at[(d + 1) * n_a + k],
             recv_sem=recv_sem.at[slot],
@@ -104,9 +92,7 @@
         for d in (-1, 1, 0):
             if d or k:
                 guarded(d, lambda d=d, k=k: block_copy(d, k).start())
-    own = pltpu.make_async_copy(
-        sendbuf.at[:, pl.ds(step * ai, chunks)], recv.at[n_a + ai], own_sem
-    )
+    own = pltpu.make_async_copy(part(ai), recv.at[n_a + ai], own_sem.at[0])
     own.start()
 
     def clear(first):
@@ -119,7 +105,8 @@
     big_row, big_col = iota((cells, cells), 0), iota((cells, cells), 1)
     same_block = (big_row // NO == big_col // NO).astype(f32).astype(bf16)
     same_place = (big_row // NO == big_col % NO).astype(f32).astype(bf16)
-    flat = coupling[...].reshape(edges, cells).astype(f32)
+    coupling_copy.wait()
+    flat = local_coupling[...].reshape(edges, cells).astype(f32)
     place = iota((edges, cells), 1) % NO
 
     def expand(j, carry):
@@ -132,7 +119,7 @@
             right[at, :] = two[:, h * LANES:(h + 1) * LANES]
         return carry
 
-    lax.fori_loop(0, NO, expand, 0)
+    lax.fori_loop(0, NO, expand, 0, unroll=4)
 
     def product(edge, carry):
         for h in range(halves):
@@ -144,7 +131,8 @@
                 ).astype(bf16)
         return carry
 
-    lax.fori_loop(0, edges, product, 0)
+    early = edges * 5 // 8
+    lax.fori_loop(0, early, product, 0, unroll=4)
 
     shape = (6 * width, 2 * span)
     row, col = iota(shape, 0), iota(shape, 1)
@@ -168,7 +156,7 @@
                 def arrive(d=d, k=k):
                     slot = (d + 1) * n_a + lax.rem(ai + k, n_a)
                     pltpu.make_async_remote_copy(
-                        src_ref=sendbuf.at[:, pl.ds(0, chunks)],
+                        src_ref=part(0),
                         dst_ref=recv.at[slot],
                         send_sem=send_sem.at[(d + 1) * n_a + k],
                         recv_sem=recv_sem.at[slot],
@@ -179,21 +167,45 @@
 
     def widen(position, carry):
         for plane in range(planes):
-            at = pl.multiple_of((position * planes + plane) * line, line)
-            framed[pl.ds(at, line), :] = recv[position, plane].reshape(line, LANES).astype(f32)
+            value = recv[position, plane // rows, plane % rows].astype(f32)
+            for h in range(halves):
+                at = pl.multiple_of((position * planes + plane) * line + h * atoms, atoms)
+                framed[pl.ds(at, atoms), :] = value[:, h * LANES:(h + 1) * LANES]
         return carry
 
     lax.fori_loop(0, 3 * n_a, widen, 0)
 
     def mix(t, carry):
-        for h in range(halves):
-            column = framed[pl.ds(2 * t + h, 2 * span, stride=line), :].astype(bf16)
-            sources[t, :, h * LANES:(h + 1) * LANES] = jnp.dot(
-                table, column, preferred_element_type=f32
-            ).astype(bf16)
-        return carry
-
-    lax.fori_loop(0, window, mix, 0)
+        column = jnp.concatenate(
+            [framed[pl.ds(h * atoms + t, 2 * span, stride=line), :] for h in range(halves)], axis=1
+        ).astype(bf16)
+        mixed = jnp.dot(table, column, preferred_element_type=f32).astype(bf16)
+        sources[REACH + t] = mixed[0:4 * width]
+        higher[t] = mixed[4 * width:]
+        return carry
+
+    has_left, has_right = ai > 0, ai < n_a - 1
+
+    def edge_copy(side):
+        start, landing = (REACH, REACH + atoms) if side == 0 else (atoms, 0)
+        return pltpu.make_async_remote_copy(
+            src_ref=sources.at[pl.ds(start, REACH)],
+            dst_ref=sources.at[pl.ds(landing, REACH)],
+            send_sem=esend.at[side],
+            recv_sem=erecv.at[side],
+            device_id=(ei, ai - 1 + 2 * side),
+            device_id_type=MESH,
+        )
+
+    lax.fori_loop(0, REACH, mix, 0, unroll=4)
+    pl.when(has_left)(lambda: edge_copy(0).start())
+    lax.fori_loop(REACH, atoms, mix, 0, unroll=4)
+    pl.when(has_right)(lambda: edge_copy(1).start())
+    lax.fori_loop(early, edges, product, 0, unroll=4)
+    pl.when(has_left)(lambda: edge_copy(0).wait_send())
+    pl.when(has_right)(lambda: edge_copy(1).wait_send())
+    pl.when(has_right)(lambda: edge_copy(0).wait_recv())
+    pl.when(has_left)(lambda: edge_copy(1).wait_recv())
 
     first = ai * atoms - REACH
     both = 2 * width
@@ -202,8 +214,8 @@
         total = jnp.zeros((both, cells), f32)
         bubbles = []
         for n in range(slots):
-            place = jnp.clip(neighbours[a, n] - first, 0, window - 1)
-            mixed = sources[place, 0:4 * width, :]
+            place = jnp.clip(neighbours[n, a] - first, 0, window - 1)
+            mixed = sources[place]
             result = jnp.dot(mixed, kron[a * slots + n], preferred_element_type=f32)
             live = jnp.where(n < counts[a], 1.0, 0.0)
             total = total + result[:both] * live
@@ -211,7 +223,7 @@
         bubble = jnp.concatenate(bubbles, axis=0).astype(bf16)
         inter[pl.ds(pl.multiple_of(a * slots * width, slots * width), slots * width), 0:both] = (
             lax.dot_general(
-                bubble, sources[REACH + a, 4 * width:6 * width, :],
+                bubble, higher[a],
                 (((1,), (1,)), ((), ())), preferred_element_type=f32,
             )
         )
@@ -222,7 +234,7 @@
         return carry
 
     inter[...] = jnp.zeros(inter.shape, f32)
-    lax.fori_loop(0, atoms, atom_step, 0)
+    lax.fori_loop(0, atoms, atom_step, 0, unroll=4)
 
     by_shift = jnp.zeros((edges, LANES), f32)
     for e in range(width):
@@ -256,9 +268,9 @@
                 parts.append(value)
             sig.append(jnp.concatenate(parts, axis=1))
         for g in range(2):
-            base = ((n_a + e // rows) * planes + g * rows + e % rows) * line + 2 * REACH
+            base = ((n_a + e // rows) * planes + g * rows + e % rows) * line
             gre.append(jnp.concatenate(
-                [framed[pl.ds(base + h, atoms, stride=2), :].astype(bf16) for h in range(halves)],
+                [framed[base + h * atoms:base + (h + 1) * atoms, :].astype(bf16) for h in range(halves)],
                 axis=1,
             ))
         outer = lax.dot_general(
@@ -342,10 +354,10 @@
     width = n_a * rows
     span = width + 2 * REACH
     window = atoms + 2 * REACH
-    chunks = window // REACH
     f32, bf16 = jnp.float32, jnp.bfloat16
     halves = cells // LANES
     vmem = pl.BlockSpec(memory_space=pltpu.VMEM)
+    hbm = pl.BlockSpec(memory_space=pltpu.HBM)
     smem = pl.BlockSpec(memory_space=pltpu.SMEM)
     dma = pltpu.SemaphoreType.DMA
     return pl.pallas_call(
@@ -355,17 +367,17 @@
             jax.ShapeDtypeStruct((atoms, slots * offsets.shape[0]), f32),
             jax.ShapeDtypeStruct((rows, cells), f32),
         ),
-        in_specs=[vmem, vmem, smem, smem, smem, smem],
+        in_specs=[hbm, hbm, smem, smem, smem, smem],
         out_specs=(vmem, vmem, vmem),
         scratch_shapes=[
-            pltpu.VMEM((2 * rows * 2 * all_atoms, LANES), f32),
-            pltpu.VMEM((2 * rows, all_atoms // REACH + 2, 2 * REACH, LANES), bf16),
-            pltpu.VMEM((3 * n_a, 2 * rows, chunks, 2 * REACH, LANES), bf16),
-            pltpu.VMEM((2 * span * 2 * window, LANES), f32),
+            pltpu.VMEM(coupling.shape, bf16),
+            pltpu.VMEM((3 * n_a, 2, rows, atoms, cells), bf16),
+            pltpu.VMEM((2 * span * halves * atoms, LANES), f32),
             pltpu.VMEM((halves * NO * edges, LANES), f32),
             pltpu.VMEM((halves * NO * edges, LANES), f32),
             pltpu.VMEM((edges, cells, cells), bf16),
-            pltpu.VMEM((window, 6 * width, cells), bf16),
+            pltpu.VMEM((window, 4 * width, cells), bf16),
+            pltpu.VMEM((atoms, 2 * width, cells), bf16),
             pltpu.VMEM((halves * 2 * width * atoms, LANES), f32),
             pltpu.VMEM((edges * width, LANES), f32),
             pltpu.VMEM((width * NO, cells), f32),
@@ -373,13 +385,13 @@
             pltpu.VMEM((n_e, REACH, edges), f32),
             pltpu.VMEM((width, cells), f32),
             pltpu.VMEM((n_a, width, cells), f32),
-            dma((3 * n_a,)), dma((3 * n_a,)), dma,
+            dma((3 * n_a,)), dma((3 * n_a,)), dma((2,)), dma((2,)), dma((2,)),
             dma((n_e,)), dma((n_e,)), dma((n_a,)), dma((n_a,)),
         ],
         compiler_params=pltpu.CompilerParams(
-            collective_id=0, has_side_effects=True, vmem_limit_bytes=48 * 1024 * 1024
+            collective_id=0, has_side_effects=True, vmem_limit_bytes=63 * 1024 * 1024
         ),
-    )(greens, coupling, neighbours, counts, phonon_weights, offsets)
+    )(greens, coupling, neighbours.T, counts, phonon_weights, offsets)
 
 
 def solution(mesh):

time: 40.7 us -> 30.4 us (0.75)
  Pallas kernels: 35.5 us -> 26.4 us
  local copies, waits for them, and re-layouts: 4.36 us -> 2.82 us
    pallas_call x1, Pallas kernels: 35.5 us -> 26.4 us  [shards(): pl.pallas_call(functools.partial(kernel, n_e, n_a), out_shape=(jax.ShapeD...]
    unnamed x14 -> x7, local copies, waits for them, and re-layouts: 4.36 us -> 2.82 us
where the time goes in v2:
time: 30.4 us; the launch traced here: 29.8 us
  Pallas kernels  26.4 us (87%)
  local copies, waits for them, and re-layouts  2.82 us (9%)
  between operations  0.65 us (2%)
    pallas_call x1, Pallas kernels, shards(): pl.pallas_call(functools.partial(kernel, n_e, n_a), out_shape=(jax.ShapeD...  26.4 us
    unnamed x7, local copies, waits for them, and re-layouts  2.82 us

profile of v2, /device:TPU:0, one launch (start us, length us, event | category | flops | bytes accessed | tf_op | source)
XLA Modules:
  0.0 29.8 jit_solution(2435524698600670252)
XLA Ops:
  0.6 26.4 %shard_map.85 = (bf16[2,8,16,256]{3,2,1,0:T(8,128)(2,1)}, f32[16,128]{1,0:T(8,128)}, f32[2,256]{1,0:T(2,128)}) custom-call(bf16[2,2,64,256]{3,2,1,0:T(8,128)(2,1)} %greens.1, bf16[16,8,256]{2,1,0:T(8,128)(2,1)} %coupling.1, s32[8,16]{1,0:T(8,128)} %bitcast.1, s32[16]{0:T(128)} %counts.1, f32[2,16]{1,0:T(2,128)} %weights.1, s32[16]{0:T(128)} %offsets.1), custom_call_target="tpu_custom_call" | custom-call | tf_op jit(solution)/shard_map/pallas_call | solution.py:363
  27.0 0.0 copy-start
  27.0 1.6 %copy.12 = bf16[2,8,16,256]{3,2,1,0:T(8,128)(2,1)} copy(bf16[2,8,16,256]{3,2,1,0:T(8,128)(2,1)} %get-tuple-element.6) | data formatting | bytes 262144
  28.6 0.0 copy-done
  28.6 0.0 copy-start.1
  28.6 0.6 %copy.13 = f32[16,128]{1,0:T(8,128)} copy(f32[16,128]{1,0:T(8,128)S(1)} %copy-done) | data formatting | bytes 16384
  29.2 0.1 copy-done.1
  29.3 0.6 %copy.14 = f32[2,256]{1,0:T(2,128)} copy(f32[2,256]{1,0:T(2,128)S(1)} %copy-done.1) | data formatting | bytes 4096
Async XLA Ops:
  27.0 1.6 %copy-start = (f32[16,128]{1,0:T(8,128)S(1)}, f32[16,128]{1,0:T(8,128)}, u32[]{:S(2)}) copy-start(f32[16,128]{1,0:T(8,128)} %get-tuple-element.7) | copy-start | bytes 24580
  28.6 0.7 %copy-start.1 = (f32[2,256]{1,0:T(2,128)S(1)}, f32[2,256]{1,0:T(2,128)}, u32[]{:S(2)}) copy-start(f32[2,256]{1,0:T(2,128)} %get-tuple-element.8) | copy-start | bytes 6148

commit v3 on v2

--- a/solution.py
+++ b/solution.py
@@ -20,9 +20,9 @@
 
 def kernel(
     n_e, n_a,
-    greens, coupling, neighbours, counts, weights, offsets,
+    greens, coupling, neighbours_in, counts_in, weights_in, offsets_in,
     sigma_out, phonon_out, current_out,
-    local_coupling, recv, framed, left, right, kron, sources, higher,
+    neighbours, counts, weights, offsets, local_coupling, recv, framed, left, right, kron, sources, higher,
     sums, inter, pre, mine_p, got_p, mine_c, got_c,
     send_sem, recv_sem, own_sem, esend, erecv, psend, precv, csend, crecv,
 ):
@@ -50,6 +50,18 @@
         else:
             pl.when(ok(d))(body)
 
+    coupling_copy = pltpu.make_async_copy(coupling, local_coupling, own_sem.at[1])
+    coupling_copy.start()
+    small = [
+        pltpu.make_async_copy(source, target, own_sem.at[2 + i])
+        for i, (source, target) in enumerate(
+            [(neighbours_in, neighbours), (counts_in, counts),
+             (weights_in, weights), (offsets_in, offsets)]
+        )
+    ]
+    for copy in small:
+        copy.start()
+
     barrier = pltpu.get_barrier_semaphore()
 
     def greet(e, a):
@@ -67,11 +79,25 @@
 
     lax.fori_loop(1, n_e, greet_far, 0)
 
+    shape = (6 * width, 2 * span)
+    row, col = iota(shape, 0), iota(shape, 1)
+    kind = row // width
+    half = (col // rows) % 2
+    energy = (col // planes) * rows + col % rows
+    distance = energy - row % width - REACH
+    shift = jnp.where(kind == 0, distance, -distance)
+    for copy in small:
+        copy.wait()
+    coef = jnp.zeros(shape, f32)
+    for w in range(offsets.shape[0]):
+        coef = coef + jnp.where(shift == offsets[w], weights[0, w], 0.0)
+        coef = coef + jnp.where(shift == -offsets[w], weights[1, w], 0.0)
+    middle = jnp.where((kind == 2) & (half == 1) & (distance == 0), 1.0, 0.0)
+    above = jnp.where((kind >= 4) & (half == 0) & (energy - REACH == row - 4 * width), 1.0, 0.0)
+    table = jnp.where((kind < 2) & (kind == half), coef, middle + above).astype(bf16)
+
     near = lower.astype(jnp.int32) + upper.astype(jnp.int32)
     pl.semaphore_wait(barrier, n_a - 1 + n_a * near + (n_e - 1 - near))
-
-    coupling_copy = pltpu.make_async_copy(coupling, local_coupling, own_sem.at[1])
-    coupling_copy.start()
 
     def part(other):
         return greens.at[:, :, pl.ds(pl.multiple_of(other * atoms, atoms), atoms), :]
@@ -133,21 +159,6 @@
 
     early = edges * 5 // 8
     lax.fori_loop(0, early, product, 0, unroll=4)
-
-    shape = (6 * width, 2 * span)
-    row, col = iota(shape, 0), iota(shape, 1)
-    kind = row // width
-    half = (col // rows) % 2
-    energy = (col // planes) * rows + col % rows
-    distance = energy - row % width - REACH
-    shift = jnp.where(kind == 0, distance, -distance)
-    coef = jnp.zeros(shape, f32)
-    for w in range(offsets.shape[0]):
-        coef = coef + jnp.where(shift == offsets[w], weights[0, w], 0.0)
-        coef = coef + jnp.where(shift == -offsets[w], weights[1, w], 0.0)
-    middle = jnp.where((kind == 2) & (half == 1) & (distance == 0), 1.0, 0.0)
-    above = jnp.where((kind >= 4) & (half == 0) & (energy - REACH == row - 4 * width), 1.0, 0.0)
-    table = jnp.where((kind < 2) & (kind == half), coef, middle + above).astype(bf16)
 
     own.wait()
     for d in (-1, 0, 1):
@@ -234,7 +245,7 @@
         return carry
 
     inter[...] = jnp.zeros(inter.shape, f32)
-    lax.fori_loop(0, atoms, atom_step, 0, unroll=4)
+    lax.fori_loop(0, atoms, atom_step, 0, unroll=16)
 
     by_shift = jnp.zeros((edges, LANES), f32)
     for e in range(width):
@@ -347,6 +358,12 @@
     current_out[...] = own_rows
 
 
+def hand_over(a, b, c, x, y, z):
+    x[...] = a[...]
+    y[...] = b[...]
+    z[...] = c[...]
+
+
 def shards(n_e, n_a, greens, coupling, neighbours, counts, phonon_weights, offsets):
     _, rows, all_atoms, cells = greens.shape
     atoms, slots = neighbours.shape
@@ -358,18 +375,21 @@
     halves = cells // LANES
     vmem = pl.BlockSpec(memory_space=pltpu.VMEM)
     hbm = pl.BlockSpec(memory_space=pltpu.HBM)
-    smem = pl.BlockSpec(memory_space=pltpu.SMEM)
     dma = pltpu.SemaphoreType.DMA
-    return pl.pallas_call(
+    results = pl.pallas_call(
         functools.partial(kernel, n_e, n_a),
         out_shape=(
             jax.ShapeDtypeStruct((2, width, atoms, cells), bf16),
             jax.ShapeDtypeStruct((atoms, slots * offsets.shape[0]), f32),
             jax.ShapeDtypeStruct((rows, cells), f32),
         ),
-        in_specs=[hbm, hbm, smem, smem, smem, smem],
+        in_specs=[hbm] * 6,
         out_specs=(vmem, vmem, vmem),
         scratch_shapes=[
+            pltpu.SMEM((slots, atoms), jnp.int32),
+            pltpu.SMEM(counts.shape, jnp.int32),
+            pltpu.SMEM(phonon_weights.shape, f32),
+            pltpu.SMEM(offsets.shape, jnp.int32),
             pltpu.VMEM(coupling.shape, bf16),
             pltpu.VMEM((3 * n_a, 2, rows, atoms, cells), bf16),
             pltpu.VMEM((2 * span * halves * atoms, LANES), f32),
@@ -385,13 +405,19 @@
             pltpu.VMEM((n_e, REACH, edges), f32),
             pltpu.VMEM((width, cells), f32),
             pltpu.VMEM((n_a, width, cells), f32),
-            dma((3 * n_a,)), dma((3 * n_a,)), dma((2,)), dma((2,)), dma((2,)),
+            dma((3 * n_a,)), dma((3 * n_a,)), dma((6,)), dma((2,)), dma((2,)),
             dma((n_e,)), dma((n_e,)), dma((n_a,)), dma((n_a,)),
         ],
         compiler_params=pltpu.CompilerParams(
             collective_id=0, has_side_effects=True, vmem_limit_bytes=63 * 1024 * 1024
         ),
     )(greens, coupling, neighbours.T, counts, phonon_weights, offsets)
+    return pl.pallas_call(
+        hand_over,
+        out_shape=tuple(jax.ShapeDtypeStruct(r.shape, r.dtype) for r in results),
+        in_specs=[vmem] * 3,
+        out_specs=(vmem,) * 3,
+    )(*results)
 
 
 def solution(mesh):

time: 30.4 us -> 27.6 us (0.908)
  local copies, waits for them, and re-layouts: 2.82 us -> 0 us
    unnamed x7 -> x0, local copies, waits for them, and re-layouts: 2.82 us -> none
    pallas_call x0 -> x1, Pallas kernels: none -> 1.59 us  [shards(): pl.pallas_call(hand_over, out_shape=tuple((jax.ShapeDtypeStruct(r.shape,...]
    pallas_call x1, Pallas kernels: 26.4 us -> 24.9 us  [shards(): pl.pallas_call(functools.partial(kernel, n_e, n_a), out_shape=(jax.ShapeD...]
where the time goes in v3:
time: 27.6 us; the launch traced here: 27.1 us
  Pallas kernels  26.5 us (96%)
  between operations  0.64 us (2%)
    pallas_call x1, Pallas kernels, shards(): pl.pallas_call(functools.partial(kernel, n_e, n_a), out_shape=(jax.ShapeD...  24.9 us
    pallas_call x1, Pallas kernels, shards(): pl.pallas_call(hand_over, out_shape=tuple((jax.ShapeDtypeStruct(r.shape,...  1.59 us

profile of v3, /device:TPU:0, one launch (start us, length us, event | category | flops | bytes accessed | tf_op | source)
XLA Modules:
  0.0 27.1 jit_solution(3492965015759229824)
XLA Ops:
  0.6 24.9 %shard_map.85 = (bf16[2,8,16,256]{3,2,1,0:T(8,128)(2,1)}, f32[16,128]{1,0:T(8,128)}, f32[2,256]{1,0:T(2,128)}) custom-call(bf16[2,2,64,256]{3,2,1,0:T(8,128)(2,1)} %greens.1, bf16[16,8,256]{2,1,0:T(8,128)(2,1)} %coupling.1, s32[8,16]{1,0:T(8,128)} %bitcast.1, s32[16]{0:T(128)} %counts_in.1, f32[2,16]{1,0:T(2,128)} %weights_in.1, s32[16]{0:T(128)} %offsets_in.1), custom_call_target="tpu_custom_call" | custom-call | tf_op jit(solution)/shard_map/pallas_call | solution.py:379
  25.5 1.6 %shard_map.86 = (bf16[2,8,16,256]{3,2,1,0:T(8,128)(2,1)}, f32[16,128]{1,0:T(8,128)}, f32[2,256]{1,0:T(2,128)}) custom-call(bf16[2,8,16,256]{3,2,1,0:T(8,128)(2,1)} %get-tuple-element.6.a, f32[16,128]{1,0:T(8,128)} %get-tuple-element.7.b, f32[2,256]{1,0:T(2,128)} %get-tuple-element.8.c), custom_call_target="tpu_custom_call" | custom-call | tf_op jit(solution)/shard_map/pallas_call | solution.py:415
